TPU v7x, 32 devices: a whole 2x2x4 slice. The times are simulated.
32 devices in a mesh: dp: 8 (over y, x, core), table: 4 (over z).
Axes of the slice: x: 2, y: 2, z: 4, core: 2. Of those that a mesh axis runs over, the one named last changes fastest.
Arguments:
- knowledge: bfloat16 [5, 4608, 768], P(None, ('dp', 'table')), may hold values from -2.390625 to 2.390625
- expr_table: bfloat16 [128, 768], replicated, may hold values from -2.390625 to 2.390625
- gene_owner: int32 [8192, 1], P(('dp', 'table')), may hold values from 0 to 31; in each aligned block of 256 rows (0 to 255, 256 to 511, ...) at most 16 rows name the same one
- gene_row: int32 [8192], P(('dp', 'table')), may hold values from 0 to 143
- expr_bin: int32 [8192], P(('dp', 'table')), may hold values from 0 to 127
- cell_lengths: int32 [256], P(('dp', 'table')), may hold values from 0 to 256, as said below
- norm1_gain: float32 [768], replicated, may hold values from 0.5 to 1.5
- norm1_bias: float32 [768], replicated, may hold values from -1.8 to 1.8
- w_query: bfloat16 [768, 768], replicated, may hold values from -0.21875 to 0.21875
- b_query: float32 [768], replicated, may hold values from -1.8 to 1.8
- w_key: bfloat16 [768, 768], replicated, may hold values from -0.21875 to 0.21875
- w_value: bfloat16 [768, 768], replicated, may hold values from -0.21875 to 0.21875
- b_value: float32 [768], replicated, may hold values from -1.8 to 1.8
- w_attn_out: bfloat16 [768, 768], replicated, may hold values from -0.875 to 0.875
- b_attn_out: float32 [768], replicated, may hold values from -1.8 to 1.8
- norm2_gain: float32 [768], replicated, may hold values from 0.5 to 1.5
- norm2_bias: float32 [768], replicated, may hold values from -1.8 to 1.8
- w_in: bfloat16 [768, 3072], replicated, may hold values from -0.21875 to 0.21875
- b_in: float32 [3072], replicated, may hold values from -1.8 to 1.8
- w_out: bfloat16 [3072, 768], replicated, may hold values from -0.109375 to 0.109375
- b_out: float32 [768], replicated, may hold values from -1.8 to 1.8
- cotangent: bfloat16 [8192, 768], P(('dp', 'table')), may hold values from -6 to 6
Outputs:
- mixed: bfloat16 [8192, 768], P(('dp', 'table'))
- knowledge_grad: float32 [5, 4608, 768], P(None, ('dp', 'table'))
- expr_table_grad: float32 [128, 768], replicated
- norm1_gain_grad: float32 [768], replicated
- norm1_bias_grad: float32 [768], replicated
- w_query_grad: float32 [768, 768], replicated
- b_query_grad: float32 [768], replicated
- w_key_grad: float32 [768, 768], replicated
- w_value_grad: float32 [768, 768], replicated
- b_value_grad: float32 [768], replicated
- w_attn_out_grad: float32 [768, 768], replicated
- b_attn_out_grad: float32 [768], replicated
- norm2_gain_grad: float32 [768], replicated
- norm2_bias_grad: float32 [768], replicated
- w_in_grad: float32 [768, 3072], replicated
- b_in_grad: float32 [3072], replicated
- w_out_grad: float32 [3072, 768], replicated
- b_out_grad: float32 [768], replicated
Inputs may be any that keep to these rules, and one draw needn't show every extreme that they name: `gene_owner`: within the rows of one device no owner index is named by more than 16 rows, and in every draw some device names some owner exactly 16 times. `cell_lengths`: the 8 entries of one device sum to at most 256; the first is positive and zeros stand only after the positive ones. In every draw some device holds a single cell of 256 tokens.
All inputs are finite; a program needn't handle non-finite values.
Results may differ from a plain program's by a relative error of at most 0.012.
Values may be sent and summed in bfloat16 or wider, within the bound.
A program may use at most 192 MiB of HBM per device.

v0:
```python
import jax
import jax.numpy as jnp
from jax import lax
from jax.sharding import PartitionSpec as P

HEADS = 12
HEAD_DIM = 64
TABLES = 5
LAYER_EPS = 1e-05
GELU_SLOPE = 0.7978845608028654
GELU_CUBIC = 0.044715
MASKED = -1e30


def gelu_tanh(pre_act):
    return (
        0.5
        * pre_act
        * (1.0 + jnp.tanh(GELU_SLOPE * (pre_act + GELU_CUBIC * pre_act * pre_act * pre_act)))
    )


def layer_norm(inputs, gain, shift):
    average = jnp.mean(inputs, axis=-1, keepdims=True)
    centred = inputs - average
    spread = jnp.mean(centred * centred, axis=-1, keepdims=True)
    return centred * lax.rsqrt(spread + LAYER_EPS) * gain + shift


def cell_masks(lengths, count):
    cell_ends = jnp.cumsum(lengths)
    places = jnp.arange(count, dtype=jnp.int32)
    segment = jnp.sum((places[:, None] >= cell_ends[None, :]).astype(jnp.int32), axis=1)
    live_mask = (places < cell_ends[-1]).astype(jnp.float32)
    return (segment, live_mask)


def local(
    knowledge,
    expr_table,
    gene_owner,
    gene_row,
    expr_bin,
    cell_lengths,
    norm1_gain,
    norm1_bias,
    w_query,
    b_query,
    w_key,
    w_value,
    b_value,
    w_attn_out,
    b_attn_out,
    norm2_gain,
    norm2_bias,
    w_in,
    b_in,
    w_out,
    b_out,
    cotangent,
):
    devices = lax.axis_size(("dp", "table"))
    tok_count = cotangent.shape[0]
    model_width = cotangent.shape[1]
    table_rows = knowledge.shape[1]
    capacity = 2 * tok_count // devices
    owner_ids = gene_owner[:, 0]
    owner_hot = (owner_ids[:, None] == jnp.arange(devices, dtype=jnp.int32)[None, :]).astype(
        jnp.int32
    )
    running = jnp.cumsum(owner_hot, axis=0) - owner_hot
    slot_rank = jnp.sum(running * owner_hot, axis=1)
    send_slot = owner_ids * capacity + slot_rank
    outgoing = jnp.full((devices * capacity,), -1, jnp.int32).at[send_slot].set(gene_row)
    outgoing = outgoing.reshape(devices, capacity)
    arrived = lax.all_to_all(outgoing, ("dp", "table"), split_axis=0, concat_axis=0, tiled=True)
    slot_count = arrived.shape[1]
    flat_ids = arrived.reshape(-1)
    row_hot = (flat_ids[:, None] == jnp.arange(table_rows, dtype=jnp.int32)[None, :]).astype(
        jnp.bfloat16
    )
    picked = jnp.einsum(
        "sr,krd->skd", row_hot, knowledge, preferred_element_type=jnp.float32
    ).astype(jnp.bfloat16)
    returned_rows = lax.all_to_all(
        picked.reshape(devices, slot_count, TABLES * model_width),
        ("dp", "table"),
        split_axis=0,
        concat_axis=0,
        tiled=True,
    )
    owner_hot_rows = row_hot.reshape(devices, slot_count, table_rows)
    own_rows = returned_rows.reshape(devices * capacity, returned_rows.shape[2])[send_slot]
    gene_part = jnp.sum(own_rows.reshape(tok_count, TABLES, model_width), axis=1, dtype=jnp.float32)
    expr_hot = (
        expr_bin[:, None] == jnp.arange(expr_table.shape[0], dtype=jnp.int32)[None, :]
    ).astype(jnp.bfloat16)
    embedded = gene_part + jnp.dot(expr_hot, expr_table, preferred_element_type=jnp.float32)
    segment, live_mask = cell_masks(cell_lengths, tok_count)
    normed1, norm1_back = jax.vjp(layer_norm, embedded, norm1_gain, norm1_bias)
    attn_in = normed1.astype(jnp.bfloat16)
    query_rows = (jnp.dot(attn_in, w_query, preferred_element_type=jnp.float32) + b_query).astype(
        jnp.bfloat16
    )
    key_rows = jnp.dot(attn_in, w_key, preferred_element_type=jnp.float32).astype(jnp.bfloat16)
    value_rows = (jnp.dot(attn_in, w_value, preferred_element_type=jnp.float32) + b_value).astype(
        jnp.bfloat16
    )
    block_rows = min(512, tok_count)
    block_count = tok_count // block_rows
    score_scale = HEAD_DIM ** (-0.5)
    key_heads = key_rows.reshape(tok_count, HEADS, HEAD_DIM)
    value_heads = value_rows.reshape(tok_count, HEADS, HEAD_DIM)
    query_blocks = query_rows.reshape(block_count, block_rows, HEADS, HEAD_DIM)
    segment_blocks = segment.reshape(block_count, block_rows)

    def block_scores(query_part, segment_part):
        scores = (
            jnp.einsum("qhd,khd->hqk", query_part, key_heads, preferred_element_type=jnp.float32)
            * score_scale
        )
        same_cell = segment_part[:, None] == segment[None, :]
        return jnp.where(same_cell[None], scores, MASKED)

    def attend_forward(inputs):
        query_part, segment_part = inputs
        scores = block_scores(query_part, segment_part)
        row_max = jnp.max(scores, axis=-1, keepdims=True)
        exp_scores = jnp.exp(scores - row_max)
        row_total = jnp.sum(exp_scores, axis=-1, keepdims=True)
        attn_probs = (exp_scores / row_total).astype(jnp.bfloat16)
        context_part = jnp.einsum(
            "hqk,khd->qhd", attn_probs, value_heads, preferred_element_type=jnp.float32
        )
        return (context_part.astype(jnp.bfloat16), row_max + jnp.log(row_total))

    context_blocks, log_totals = lax.map(attend_forward, (query_blocks, segment_blocks))
    context = context_blocks.reshape(tok_count, model_width)
    attended = jnp.dot(context, w_attn_out, preferred_element_type=jnp.float32) + b_attn_out
    hidden1 = embedded + attended
    normed2, norm2_back = jax.vjp(layer_norm, hidden1, norm2_gain, norm2_bias)
    ffn_in = normed2.astype(jnp.bfloat16)
    pre_act = jnp.dot(ffn_in, w_in, preferred_element_type=jnp.float32) + b_in
    activated, gelu_back = jax.vjp(gelu_tanh, pre_act)
    act_low = activated.astype(jnp.bfloat16)
    hidden2 = hidden1 + jnp.dot(act_low, w_out, preferred_element_type=jnp.float32) + b_out
    mixed = (hidden2 * live_mask[:, None]).astype(jnp.bfloat16)
    grad_hidden2 = cotangent.astype(jnp.float32) * live_mask[:, None]
    grad_ffn = grad_hidden2.astype(jnp.bfloat16)
    b_out_grad = jnp.sum(grad_ffn, axis=0, dtype=jnp.float32)
    w_out_grad = jnp.einsum("tf,td->fd", act_low, grad_ffn, preferred_element_type=jnp.float32)
    grad_act = jnp.einsum("td,fd->tf", grad_ffn, w_out, preferred_element_type=jnp.float32)
    grad_pre = gelu_back(grad_act)[0].astype(jnp.bfloat16)
    b_in_grad = jnp.sum(grad_pre, axis=0, dtype=jnp.float32)
    w_in_grad = jnp.einsum("td,tf->df", ffn_in, grad_pre, preferred_element_type=jnp.float32)
    grad_normed2 = jnp.einsum("tf,df->td", grad_pre, w_in, preferred_element_type=jnp.float32)
    grad_from2, norm2_gain_grad, norm2_bias_grad = norm2_back(grad_normed2)
    grad_hidden1 = grad_hidden2 + grad_from2
    grad_attn = grad_hidden1.astype(jnp.bfloat16)
    b_attn_out_grad = jnp.sum(grad_attn, axis=0, dtype=jnp.float32)
    w_attn_out_grad = jnp.einsum(
        "td,te->de", context, grad_attn, preferred_element_type=jnp.float32
    )
    grad_context = jnp.einsum(
        "te,de->td", grad_attn, w_attn_out, preferred_element_type=jnp.float32
    ).astype(jnp.bfloat16)
    grad_blocks = grad_context.reshape(block_count, block_rows, HEADS, HEAD_DIM)

    def attend_backward(carry, inputs):
        key_sum, value_sum = carry
        query_part, segment_part, log_part, grad_part = inputs
        scores = block_scores(query_part, segment_part)
        attn_probs = jnp.exp(scores - log_part)
        grad_probs = jnp.einsum(
            "qhd,khd->hqk", grad_part, value_heads, preferred_element_type=jnp.float32
        )
        value_sum = value_sum + jnp.einsum(
            "hqk,qhd->khd",
            attn_probs.astype(jnp.bfloat16),
            grad_part,
            preferred_element_type=jnp.float32,
        )
        grad_scores = attn_probs * (
            grad_probs - jnp.sum(attn_probs * grad_probs, axis=-1, keepdims=True)
        )
        grad_scores = grad_scores.astype(jnp.bfloat16)
        grad_query_part = (
            jnp.einsum("hqk,khd->qhd", grad_scores, key_heads, preferred_element_type=jnp.float32)
            * score_scale
        )
        key_sum = (
            key_sum
            + jnp.einsum(
                "hqk,qhd->khd", grad_scores, query_part, preferred_element_type=jnp.float32
            )
            * score_scale
        )
        return ((key_sum, value_sum), grad_query_part.astype(jnp.bfloat16))

    zero_heads = jnp.zeros((tok_count, HEADS, HEAD_DIM), jnp.float32)
    (key_sum, value_sum), grad_query_blocks = lax.scan(
        attend_backward,
        (zero_heads, zero_heads),
        (query_blocks, segment_blocks, log_totals, grad_blocks),
    )
    grad_query = grad_query_blocks.reshape(tok_count, model_width)
    grad_keys = key_sum.reshape(tok_count, model_width).astype(jnp.bfloat16)
    grad_values = value_sum.reshape(tok_count, model_width).astype(jnp.bfloat16)
    w_query_grad = jnp.einsum("td,te->de", attn_in, grad_query, preferred_element_type=jnp.float32)
    b_query_grad = jnp.sum(grad_query, axis=0, dtype=jnp.float32)
    w_key_grad = jnp.einsum("td,te->de", attn_in, grad_keys, preferred_element_type=jnp.float32)
    w_value_grad = jnp.einsum("td,te->de", attn_in, grad_values, preferred_element_type=jnp.float32)
    b_value_grad = jnp.sum(grad_values, axis=0, dtype=jnp.float32)
    grad_normed1 = jnp.einsum("te,de->td", grad_query, w_query, preferred_element_type=jnp.float32)
    grad_normed1 = grad_normed1 + jnp.einsum(
        "te,de->td", grad_keys, w_key, preferred_element_type=jnp.float32
    )
    grad_normed1 = grad_normed1 + jnp.einsum(
        "te,de->td", grad_values, w_value, preferred_element_type=jnp.float32
    )
    grad_from1, norm1_gain_grad, norm1_bias_grad = norm1_back(grad_normed1)
    grad_embedded = (grad_hidden1 + grad_from1).astype(jnp.bfloat16)
    expr_table_grad = jnp.einsum(
        "tb,td->bd", expr_hot, grad_embedded, preferred_element_type=jnp.float32
    )
    outgoing_grads = (
        jnp.zeros((devices * capacity, model_width), jnp.bfloat16).at[send_slot].set(grad_embedded)
    )
    arrived_grads = lax.all_to_all(
        outgoing_grads.reshape(devices, capacity, model_width),
        ("dp", "table"),
        split_axis=0,
        concat_axis=0,
        tiled=True,
    )
    table_grad = jnp.einsum(
        "gsr,gsd->rd", owner_hot_rows, arrived_grads, preferred_element_type=jnp.float32
    )
    knowledge_grad = jnp.broadcast_to(table_grad[None], (TABLES, table_rows, model_width))
    summed = lax.psum(
        (
            w_in_grad,
            b_in_grad,
            w_out_grad,
            b_out_grad,
            norm2_gain_grad,
            norm2_bias_grad,
            norm1_gain_grad,
            norm1_bias_grad,
            w_query_grad,
            b_query_grad,
            w_key_grad,
            w_value_grad,
            b_value_grad,
            w_attn_out_grad,
            b_attn_out_grad,
            expr_table_grad,
        ),
        ("dp", "table"),
    )
    ffn_terms = summed[:6]
    attn_terms = summed[6:]
    return (
        mixed,
        knowledge_grad,
        attn_terms[9],
        attn_terms[0],
        attn_terms[1],
        attn_terms[2],
        attn_terms[3],
        attn_terms[4],
        attn_terms[5],
        attn_terms[6],
        attn_terms[7],
        attn_terms[8],
        ffn_terms[4],
        ffn_terms[5],
        ffn_terms[0],
        ffn_terms[1],
        ffn_terms[2],
        ffn_terms[3],
    )


def solution(mesh):
    in_specs = (
        P(None, ("dp", "table"), None),
        P(),
        P(("dp", "table"), None),
        P(("dp", "table")),
        P(("dp", "table")),
        P(("dp", "table")),
        P(),
        P(),
        P(),
        P(),
        P(),
        P(),
        P(),
        P(),
        P(),
        P(),
        P(),
        P(),
        P(),
        P(),
        P(),
        P(("dp", "table"), None),
    )
    out_specs = (
        P(("dp", "table"), None),
        P(None, ("dp", "table"), None),
        P(),
        P(),
        P(),
        P(),
        P(),
        P(),
        P(),
        P(),
        P(),
        P(),
        P(),
        P(),
        P(),
        P(),
        P(),
        P(),
    )
    return jax.shard_map(local, mesh=mesh, in_specs=in_specs, out_specs=out_specs, check_vma=False)
```

profile of v0, /device:TPU:0, one launch (start us, length us, event | category | flops | bytes accessed | tf_op | source)
XLA Modules:
  0.0 698.4 jit_solution(7294578656699365862)
XLA Ops:
  7.2 0.8 fusion.39
  8.0 0.6 reduce-window.10
  8.8 0.8 fusion.38
  9.6 0.7 compare_select_fusion
  10.3 1.6 scatter_custom_fusion
  11.9 14.3 %all_to_all.19 = s32[32,1,16]{2,1,0:T(1,128)S(1)} all-to-all(s32[32,1,16]{2,1,0:T(1,128)S(1)} %bitcast.118), channel_id=1, replica_groups=mesh['dp'=8,'table'=4] {'dp','table'}, dimensions={0} | all-to-all | bytes 4096 | tf_op jit(solution)/shard_map/all_to_all | solution.py:76
  26.2 0.5 broadcast.230
  26.7 0.7 reduce.8
  27.5 2.6 convolution_convert_fusion
  30.0 5.2 copy.82
  35.2 9.8 %reshape.233 = bf16[32,16,3840]{2,1,0:T(8,128)(2,1)} reshape(bf16[512,5,768]{2,1,0:T(8,128)(2,1)} %copy.82) | data formatting | bytes 7864320 | tf_op jit(solution)/shard_map/reshape | solution.py:86
  45.0 3.7 all-to-all-start.1
  49.0 0.6 slice.12
  49.6 1.2 compare_convert_fusion
  50.8 0.7 broadcast_compare_fusion
  51.6 84.0 %all-to-all-done.1 = bf16[32,16,3840]{2,1,0:T(8,128)(2,1)} async-done(((bf16[32,16,3840]{2,1,0:T(8,128)(2,1)}), bf16[32,16,3840]{2,1,0:T(8,128)(2,1)}, u32[]{:S(2)}, u32[]{:S(2)}) %all-to-all-start.1) | async-done | bytes 3932192 | tf_op jit(solution)/shard_map/all_to_all | solution.py:85
  135.5 6.4 gather_fusion
  141.9 3.2 copy.83
  145.1 2.5 reduce_sum.240
  149.9 1.9 fusion.16
  152.0 1.2 fusion.15
  153.2 1.2 copy.85
  154.4 1.6 fusion.55
  156.5 0.7 fusion.17
  157.7 1.5 copy-done.9
  159.1 0.6 fusion.56
  160.1 1.5 convolution_add_fusion
  161.7 5.4 convert_reduce_fusion
  167.1 2.3 multiply_reduce_fusion.1
  169.8 0.9 copy-done.3
  170.6 0.8 convert_reduce_fusion.2
  171.4 1.3 convolution_convert_fusion.1
  172.7 1.9 fusion.61
  174.6 1.9 copy.90
  176.5 3.4 convert_reduce_fusion.3
  180.0 0.8 multiply_reduce_fusion
  180.8 0.7 multiply_convert_fusion
  181.8 0.6 fusion.22
  182.4 0.5 convert_reduce_fusion.4
  183.1 0.5 fusion.57
  183.6 1.9 fusion.58
  185.6 6.0 fusion.44
  191.6 5.3 fusion.50
  197.0 1.9 fusion.60
  198.9 1.9 fusion.59
  200.8 0.5 convolution_add_fusion.2
  201.4 1.0 multiply_reduce_fusion.2
  203.1 1.1 fusion.33
  204.3 2.7 scatter_custom_fusion.1
  207.0 5.4 all-to-all-start.2
  212.7 50.9 %all-reduce = (f32[768]{0:T(1024)}, f32[768]{0:T(1024)}, f32[768]{0:T(1024)}, f32[768]{0:T(1024)}, f32[768]{0:T(1024)}, /*index=5*/f32[768]{0:T(1024)}, f32[768]{0:T(1024)}, f32[3072]{0:T(1024)}, f32[768]{0:T(1024)}) all-reduce(f32[768]{0:T(1024)S(1)} %get-tuple-element.77, ...), channel_id=1, replica_groups=mesh['dp'=8,'table'=4] {'dp','table'}, use_global_device_ids=true, to_apply=%region_21.22 | all-reduce | flops 9216 | bytes 73728 | tf_op jit(solution)/shard_map/psum | solution.py:240
  263.5 6.3 fusion.23
  269.8 0.5 convolution_bitcast_fusion
  270.3 396.6 %all-reduce.4.cloned.1.call-done = (f32[128,768]{1,0:T(8,128)}, f32[768,768]{1,0:T(8,128)}, f32[768,768]{1,0:T(8,128)}, f32[768,768]{1,0:T(8,128)}, f32[768,768]...) async-done(((f32[128,768]{1,0:T(8,128)}, f32[768,768]{1,0:T(8,128)}, f32[768,768]{1,0:T(8,128)}, f32[768,768]{1,0:T(8,128)}, f32[768,768]{1,0:T(8,128)}, ...) | async-done | bytes 28704784 | tf_op jit(solution)/shard_map/psum | solution.py:240
  667.0 1.5 broadcast_in_dim.108
  668.5 1.9 copy.110
  670.4 1.4 copy.111
  671.8 1.4 copy.112
  673.2 1.1 copy-done.17
  674.4 1.4 copy.113
  675.8 1.1 copy-done.16
  676.9 1.4 copy.114
  678.3 9.3 %copy.115 = f32[768,3072]{1,0:T(8,128)} copy(f32[768,3072]{1,0:T(8,128)} %get-tuple-element.134) | data formatting | bytes 18874368
  687.6 3.7 copy.116
  (178 shorter events, 6.1 us)
Async XLA Ops:
  7.2 144.7 %copy-start = (bf16[768,768]{1,0:T(8,128)(2,1)S(1)}, bf16[768,768]{1,0:T(8,128)(2,1)}, u32[]{:S(2)}) copy-start(bf16[768,768]{1,0:T(8,128)(2,1)} %param.33) | copy-start | bytes 3538948
  10.3 40.5 %copy-start.57 = (s32[256,1]{0,1:T(1,128)}, s32[256,1]{0,1:T(1,128)S(1)}, u32[]{:S(2)}) copy-start(s32[256,1]{0,1:T(1,128)S(1)} %compare_select_fusion) | copy-start | bytes 3076
  26.2 9.1 %copy-start.26 = (s32[32,1,16]{2,1,0:T(1,128)}, s32[32,1,16]{2,1,0:T(1,128)S(1)}, u32[]{:S(2)}) copy-start(s32[32,1,16]{2,1,0:T(1,128)S(1)} %all_to_all.19) | copy-start | bytes 6148
  45.0 3.7 copy-start.64
  45.0 90.5 %all-to-all-start.1 = ((bf16[32,16,3840]{2,1,0:T(8,128)(2,1)}), bf16[32,16,3840]{2,1,0:T(8,128)(2,1)}, u32[]{:S(2)}, u32[]{:S(2)}) async-start(bf16[32,16,3840]{2,1,0:T(8,128)(2,1)} %reshape.233), calls=%async_computation.1 | async-start | bytes 7864320 | tf_op jit(solution)/shard_map/all_to_all | solution.py:85
  48.7 618.2 %all-reduce.4.cloned.1.call-start = ((), (), s32[]{:S(2)}) async-start(), calls=%async_computation.3 | async-start | bytes 57409536 | tf_op jit(solution)/shard_map/psum | solution.py:240
  145.1 2.8 copy-start.25
  145.1 2.8 copy-start.55
  147.9 1.9 copy-start.61
  149.2 2.8 copy-start.62
  149.8 6.1 copy-start.11
  151.9 4.0 copy-start.13
  154.4 2.1 copy-start.20
  156.0 1.7 copy-start.1
  156.0 4.0 slice-start.3
  156.5 2.6 copy-start.9
  156.5 2.6 copy-start.54
  156.5 3.5 slice-start.4
  157.7 2.3 copy-start.28
  157.7 2.3 copy-start.30
  157.7 2.4 copy-start.60
  159.1 2.5 slice-start.5
  159.7 9.7 %copy-start.37 = (f32[256]{0:T(256)}, f32[256]{0:T(256)S(1)}, u32[]{:S(2)}) copy-start(f32[256]{0:T(256)S(1)} %broadcast_multiply_fusion) | copy-start | bytes 3076
  160.0 9.4 %copy-start.43 = (f32[256]{0:T(256)}, f32[256]{0:T(256)S(1)}, u32[]{:S(2)}) copy-start(f32[256]{0:T(256)S(1)} %fusion.43) | copy-start | bytes 3076
  160.0 1.6 copy-start.10
  160.0 1.6 copy-start.46
  160.1 1.6 slice-start.6
  161.6 5.4 copy-start.5
  167.1 2.3 copy-start.22
  169.7 3.0 copy-start.49
  176.5 3.5 copy-start.2
  176.5 3.5 copy-start.15
  176.5 3.5 copy-start.21
  180.8 1.6 copy-start.12
  182.9 2.7 copy-start.6
  182.9 2.7 copy-start.47
  185.5 6.1 copy-start.23
  185.5 6.1 copy-start.29
  185.5 6.1 copy-start.31
  185.6 6.1 copy-start.38
  185.6 6.1 copy-start.44
  197.0 3.9 copy-start.8
  198.9 2.5 copy-start.33
  198.9 2.5 copy-start.36
  198.9 2.5 copy-start.40
  200.8 1.6 copy-start.52
  201.4 1.4 copy-start.4
  204.2 8.2 %copy-start.27 = (s32[32,1,16]{2,1,0:T(1,128)S(1)}, s32[32,1,16]{2,1,0:T(1,128)}, u32[]{:S(2)}) copy-start(s32[32,1,16]{2,1,0:T(1,128)} %copy-done.26) | copy-start | bytes 6148
  204.2 8.3 %copy-start.34 = (f32[12,64]{1,0:T(8,128)S(1)}, f32[12,64]{1,0:T(8,128)}, u32[]{:S(2)}) copy-start(f32[12,64]{1,0:T(8,128)} %get-tuple-element.116) | copy-start | bytes 9220
  204.2 8.4 %copy-start.41 = (f32[768]{0:T(1024)S(1)}, f32[768]{0:T(1024)}, u32[]{:S(2)}) copy-start(f32[768]{0:T(1024)} %get-tuple-element.97) | copy-start | bytes 9220
  204.2 8.4 %copy-start.42 = (f32[768]{0:T(1024)S(1)}, f32[768]{0:T(1024)}, u32[]{:S(2)}) copy-start(f32[768]{0:T(1024)} %get-tuple-element.103) | copy-start | bytes 9220
  204.2 8.4 %copy-start.45 = (f32[3072]{0:T(1024)S(1)}, f32[3072]{0:T(1024)}, u32[]{:S(2)}) copy-start(f32[3072]{0:T(1024)} %get-tuple-element.118) | copy-start | bytes 36868
  204.2 8.4 %copy-start.58 = (f32[768]{0:T(1024)S(1)}, f32[768]{0:T(1024)}, u32[]{:S(2)}) copy-start(f32[768]{0:T(1024)} %get-tuple-element.64) | copy-start | bytes 9220
  204.2 8.4 %copy-start.59 = (f32[768]{0:T(1024)S(1)}, f32[768]{0:T(1024)}, u32[]{:S(2)}) copy-start(f32[768]{0:T(1024)} %get-tuple-element.79) | copy-start | bytes 9220
  204.2 59.3 %copy-start.48 = (f32[256]{0:T(256)S(1)}, f32[256]{0:T(256)}, u32[]{:S(2)}) copy-start(f32[256]{0:T(256)} %compare_convert_fusion) | copy-start | bytes 3076
  204.3 59.3 %copy-start.63 = (f32[768]{0:T(1024)S(1)}, f32[768]{0:T(1024)}, u32[]{:S(2)}) copy-start(f32[768]{0:T(1024)} %param.42) | copy-start | bytes 9220
  207.0 62.8 %all-to-all-start.2 = ((bf16[32,16,768]{2,1,0:T(8,128)(2,1)}), bf16[32,16,768]{2,1,0:T(8,128)(2,1)S(1)}, u32[]{:S(2)}, u32[]{:S(2)}) async-start(bf16[32,16,768]{2,1,0:T(8,128)(2,1)} %bitcast.25), calls=%async_computation.2 | async-start | bytes 1572864 | tf_op jit(solution)/shard_map/all_to_all | solution.py:229
  667.0 3.5 copy-start.19
  668.5 3.3 copy-start.18
  671.8 2.5 copy-start.17
  674.4 2.5 copy-start.16
  676.9 10.7 %slice-start = ((s8[9437184]{0:T(1024)(128)(4,1)}), s8[4194304]{0:T(1024)(128)(4,1)S(1)}, s32[]{:S(2)}) async-start(s8[9437184]{0:T(1024)(128)(4,1)} %bitcast.99), calls=%async_computation.4 | async-start | bytes 8388608
  678.3 9.3 %slice-start.1 = ((s8[9437184]{0:T(1024)(128)(4,1)}), s8[4194304]{0:T(1024)(128)(4,1)S(1)}, s32[]{:S(2)}) async-start(s8[9437184]{0:T(1024)(128)(4,1)} %bitcast.99), calls=%async_computation.5 | async-start | bytes 8388608
  678.3 9.3 %slice-start.2 = ((s8[9437184]{0:T(1024)(128)(4,1)}), s8[1048576]{0:T(1024)(128)(4,1)S(1)}, s32[]{:S(2)}) async-start(s8[9437184]{0:T(1024)(128)(4,1)} %bitcast.99), calls=%async_computation.6 | async-start | bytes 2097152
  (11 other events, 10.3 us)
Sparse Core Ops, SparseCore 0:
  204.4 462.5 all-reduce.3
where the time goes:
time: 707 us; the launch traced here: 698 us
  waiting for transfers between devices  481 us (68%)
  blocking collectives  65.2 us (9%)
  local copies, waits for them, and re-layouts  62.5 us (9%)
  matrix products  54.1 us (8%)
  between operations  15.1 us (2%)
  other arithmetic  11.8 us (2%)
  starting transfers between devices  9.12 us (1%)
    psum x1, waiting for transfers between devices, local(): lax.psum((w_in_grad, b_in_grad, w_out_grad, b_out_grad, norm2_gain_grad,...  397 us
    all_to_all x1, waiting for transfers between devices, local(): lax.all_to_all(picked.reshape(devices, slot_count, TABLES * model_width),...  84 us
    psum x1, blocking collectives, local(): lax.psum((w_in_grad, b_in_grad, w_out_grad, b_out_grad, norm2_gain_grad,...  50.9 us
    unnamed x151, local copies, waits for them, and re-layouts  26.8 us
    all_to_all x1, blocking collectives, local(): lax.all_to_all(outgoing, ('dp', 'table'), split_axis=0, concat_axis=0, ti...  14.3 us
  transfers between devices with their start and end apart: 3, of which 2 were waited for; matrix products, arithmetic and copies ran while one was open for 2% of the time, Pallas kernels for 0%

commit v1 on v0

--- a/solution.py
+++ b/solution.py
@@ -237,7 +237,7 @@
         "gsr,gsd->rd", owner_hot_rows, arrived_grads, preferred_element_type=jnp.float32
     )
     knowledge_grad = jnp.broadcast_to(table_grad[None], (TABLES, table_rows, model_width))
-    summed = lax.psum(
+    partial = lax.psum(
         (
             w_in_grad,
             b_in_grad,
@@ -256,8 +256,9 @@
             b_attn_out_grad,
             expr_table_grad,
         ),
-        ("dp", "table"),
-    )
+        "table",
+    )
+    summed = lax.psum(partial, "dp")
     ffn_terms = summed[:6]
     attn_terms = summed[6:]
     return (

time: 707 us -> 1570 us (2.22)
  waiting for transfers between devices: 481 us -> 1330 us
    psum x1, waiting for transfers between devices: 397 us -> 955 us  [local(): lax.psum((w_in_grad, b_in_grad, w_out_grad, b_out_grad, norm2_gain_grad,...]
    psum x0 -> x1, waiting for transfers between devices: none -> 294 us  [local(): summed = lax.psum(partial, 'dp')]
    psum x0 -> x1, blocking collectives: none -> 25.6 us  [local(): summed = lax.psum(partial, 'dp')]
    psum x1, blocking collectives: 50.9 us -> 29.7 us  [local(): lax.psum((w_in_grad, b_in_grad, w_out_grad, b_out_grad, norm2_gain_grad,...]
  transfers between devices with their start and end apart: 3 -> 4, of which waited for: 2 -> 3; matrix products, arithmetic and copies ran while one was open for 2% -> 1% of each run, Pallas kernels for 0% -> 0%
where the time goes in v1:
time: 1570 us; the launch traced here: 1560 us
  waiting for transfers between devices  1330 us (85%)
  blocking collectives  69.5 us (4%)
  local copies, waits for them, and re-layouts  65.7 us (4%)
  matrix products  54 us (3%)
    psum x1, waiting for transfers between devices, local(): lax.psum((w_in_grad, b_in_grad, w_out_grad, b_out_grad, norm2_gain_grad,...  955 us
    psum x1, waiting for transfers between devices, local(): summed = lax.psum(partial, 'dp')  294 us
    all_to_all x1, waiting for transfers between devices, local(): lax.all_to_all(picked.reshape(devices, slot_count, TABLES * model_width),...  83.9 us
  transfers between devices with their start and end apart: 4, of which 3 were waited for; matrix products, arithmetic and copies ran while one was open for 1% of the time, Pallas kernels for 0%

profile of v1, /device:TPU:0, one launch (start us, length us, event | category | flops | bytes accessed | tf_op | source)
XLA Modules:
  0.0 1556.8 jit_solution(17918385169577667618)
XLA Ops:
  7.2 0.8 fusion.39
  8.0 0.6 reduce-window.10
  8.8 0.8 fusion.38
  9.6 0.7 compare_select_fusion
  10.3 1.6 scatter_custom_fusion
  11.9 14.3 all_to_all.19
  26.7 0.7 reduce.8
  27.5 2.6 convolution_convert_fusion
  30.0 5.2 copy.82
  35.2 9.8 reshape.233
  45.0 3.7 all-to-all-start.1
  49.0 0.6 slice.12
  49.6 1.2 compare_convert_fusion
  50.8 0.7 broadcast_compare_fusion
  51.6 83.9 %all-to-all-done.1 = bf16[32,16,3840]{2,1,0:T(8,128)(2,1)} async-done(((bf16[32,16,3840]{2,1,0:T(8,128)(2,1)}), bf16[32,16,3840]{2,1,0:T(8,128)(2,1)}, u32[]{:S(2)}, u32[]{:S(2)}) %all-to-all-start.1) | async-done | bytes 3932192 | tf_op jit(solution)/shard_map/all_to_all | solution.py:85
  135.5 7.6 gather_fusion
  143.2 4.6 copy.83
  147.8 2.5 reduce_sum.240
  151.3 0.6 copy-done.51
  153.1 1.9 fusion.16
  155.2 1.2 fusion.15
  156.4 1.2 copy.85
  157.6 1.6 fusion.55
  159.8 0.7 fusion.17
  160.9 1.5 copy-done.9
  162.4 0.6 fusion.56
  163.3 1.5 convolution_add_fusion
  164.9 5.4 convert_reduce_fusion
  170.3 2.3 multiply_reduce_fusion.1
  173.0 0.9 copy-done.3
  173.9 0.8 convert_reduce_fusion.2
  174.7 1.3 convolution_convert_fusion.1
  176.0 1.9 fusion.61
  177.8 1.9 copy.90
  179.8 3.4 convert_reduce_fusion.3
  183.2 0.8 multiply_reduce_fusion
  184.1 0.7 multiply_convert_fusion
  185.0 0.6 fusion.22
  186.3 0.5 fusion.57
  186.9 1.9 fusion.58
  188.8 6.0 fusion.44
  194.9 5.3 fusion.50
  200.2 1.9 fusion.60
  202.2 1.9 fusion.59
  204.1 0.5 convolution_add_fusion.2
  204.7 1.0 multiply_reduce_fusion.2
  206.4 1.1 fusion.33
  207.5 955.4 %all-reduce.9.cloned.1.call-done = (f32[128,768]{1,0:T(8,128)}, f32[768,768]{1,0:T(8,128)}, f32[768,768]{1,0:T(8,128)}, f32[768,768]{1,0:T(8,128)}, f32[768,768]...) async-done(((f32[128,768]{1,0:T(8,128)}, f32[768,768]{1,0:T(8,128)}, f32[768,768]{1,0:T(8,128)}, f32[768,768]{1,0:T(8,128)}, f32[768,768]{1,0:T(8,128)}, ...) | async-done | bytes 28704784 | tf_op jit(solution)/shard_map/psum | solution.py:240
  1163.0 2.7 scatter_custom_fusion.1
  1165.7 3.8 all-to-all-start.2
  1169.8 29.7 %all-reduce.2 = (f32[768]{0:T(1024)S(1)}, f32[768]{0:T(1024)S(1)}, f32[768]{0:T(1024)S(1)}, f32[768]{0:T(1024)S(1)}, f32[768]{0:T(1024)S(1)}, /*index=5*/f32[768...) all-reduce(f32[768]{0:T(1024)S(1)} %get-tuple-element.77, ...), channel_id=1, replica_groups=mesh['dp'=8,'table'=4] {'table'}, use_global_device_ids=true, to_apply=%region_22.23 | all-reduce | flops 9216 | bytes 73728 | tf_op jit(solution)/shard_map/psum | solution.py:240
  1199.5 25.6 %all-reduce = (f32[768]{0:T(1024)}, f32[768]{0:T(1024)}, f32[768]{0:T(1024)}, f32[768]{0:T(1024)}, f32[768]{0:T(1024)}, /*index=5*/f32[768]{0:T(1024)}, f32[768]{0:T(1024)}, f32[3072]{0:T(1024)}, f32[768]{0:T(1024)}) all-reduce(f32[768]{0:T(1024)S(1)} %get-tuple-element.97, ...), channel_id=1, replica_groups=mesh['dp'=8,'table'=4] {'dp'}, use_global_device_ids=true, to_apply=%region_23.24 | all-reduce | flops 9216 | bytes 73728 | tf_op jit(solution)/shard_map/psum | solution.py:261
  1225.1 6.1 fusion.23
  1231.8 293.6 %all-reduce.7.cloned.1.call-done = (f32[128,768]{1,0:T(8,128)}, f32[768,768]{1,0:T(8,128)}, f32[768,768]{1,0:T(8,128)}, f32[768,768]{1,0:T(8,128)}, f32[768,768]...) async-done(((f32[128,768]{1,0:T(8,128)}, f32[768,768]{1,0:T(8,128)}, f32[768,768]{1,0:T(8,128)}, f32[768,768]{1,0:T(8,128)}, f32[768,768]{1,0:T(8,128)}, ...) | async-done | bytes 28704784 | tf_op jit(solution)/shard_map/psum | solution.py:261
  1525.3 1.5 broadcast_in_dim.108
  1526.9 1.9 copy.117
  1528.8 1.4 copy.118
  1530.2 1.4 copy.119
  1531.6 1.1 copy-done.17
  1532.7 1.4 copy.120
  1534.1 1.1 copy-done.16
  1535.2 1.4 copy.121
  1536.6 9.3 copy.122
  1546.0 3.7 copy.123
  (182 shorter events, 7.6 us)
Async XLA Ops:
  7.2 148.0 %copy-start = (bf16[768,768]{1,0:T(8,128)(2,1)S(1)}, bf16[768,768]{1,0:T(8,128)(2,1)}, u32[]{:S(2)}) copy-start(bf16[768,768]{1,0:T(8,128)(2,1)} %param.33) | copy-start | bytes 3538948
  10.3 40.5 %copy-start.57 = (s32[256,1]{0,1:T(1,128)}, s32[256,1]{0,1:T(1,128)S(1)}, u32[]{:S(2)}) copy-start(s32[256,1]{0,1:T(1,128)S(1)} %compare_select_fusion) | copy-start | bytes 3076
  26.2 9.1 copy-start.26
  45.0 3.7 copy-start.64
  45.0 90.5 %all-to-all-start.1 = ((bf16[32,16,3840]{2,1,0:T(8,128)(2,1)}), bf16[32,16,3840]{2,1,0:T(8,128)(2,1)}, u32[]{:S(2)}, u32[]{:S(2)}) async-start(bf16[32,16,3840]{2,1,0:T(8,128)(2,1)} %reshape.233), calls=%async_computation.1 | async-start | bytes 7864320 | tf_op jit(solution)/shard_map/all_to_all | solution.py:85
  48.7 1114.2 %all-reduce.9.cloned.1.call-start = ((), (), s32[]{:S(2)}) async-start(), calls=%async_computation.4 | async-start | bytes 57409536 | tf_op jit(solution)/shard_map/psum | solution.py:240
  147.8 2.8 copy-start.25
  147.8 2.8 copy-start.55
  150.6 1.8 copy-start.7
  150.6 2.4 copy-start.61
  152.4 2.8 copy-start.62
  153.1 6.1 copy-start.11
  155.2 4.0 copy-start.13
  157.6 2.1 copy-start.20
  159.2 1.7 copy-start.1
  159.3 4.0 slice-start.3
  159.7 2.6 copy-start.9
  159.8 2.6 copy-start.54
  159.8 3.5 slice-start.4
  160.9 2.3 copy-start.28
  160.9 2.3 copy-start.30
  160.9 2.3 copy-start.60
  162.4 2.4 slice-start.5
  163.0 9.7 copy-start.37
  163.3 9.4 copy-start.43
  163.3 1.6 copy-start.10
  163.3 1.6 slice-start.6
  164.9 5.4 copy-start.5
  170.3 2.3 copy-start.22
  173.0 3.0 copy-start.49
  179.8 3.5 copy-start.2
  179.8 3.5 copy-start.15
  179.8 3.5 copy-start.21
  184.0 1.6 copy-start.12
  186.1 2.7 copy-start.6
  186.1 2.7 copy-start.47
  188.8 6.1 copy-start.23
  188.8 6.1 copy-start.29
  188.8 6.1 copy-start.31
  188.8 6.1 copy-start.38
  188.8 6.1 copy-start.44
  200.2 3.9 copy-start.8
  202.1 2.5 copy-start.33
  202.1 2.5 copy-start.36
  202.1 2.5 copy-start.40
  204.1 1.6 copy-start.52
  207.5 1317.8 %all-reduce.7.cloned.1.call-start = ((), (), s32[]{:S(2)}) async-start(), calls=%async_computation.3 | async-start | bytes 57409536 | tf_op jit(solution)/shard_map/psum | solution.py:261
  1162.9 6.6 copy-start.27
  1162.9 6.7 copy-start.34
  1162.9 6.9 copy-start.41
  1162.9 6.9 copy-start.42
  1162.9 6.9 copy-start.45
  1163.0 6.8 copy-start.58
  1163.0 6.8 copy-start.59
  1163.0 62.1 %copy-start.48 = (f32[256]{0:T(256)S(1)}, f32[256]{0:T(256)}, u32[]{:S(2)}) copy-start(f32[256]{0:T(256)} %compare_convert_fusion) | copy-start | bytes 3076
  1163.0 62.1 %copy-start.63 = (f32[768]{0:T(1024)S(1)}, f32[768]{0:T(1024)}, u32[]{:S(2)}) copy-start(f32[768]{0:T(1024)} %param.42) | copy-start | bytes 9220
  1165.7 65.5 %all-to-all-start.2 = ((bf16[32,16,768]{2,1,0:T(8,128)(2,1)}), bf16[32,16,768]{2,1,0:T(8,128)(2,1)S(1)}, u32[]{:S(2)}, u32[]{:S(2)}) async-start(bf16[32,16,768]{2,1,0:T(8,128)(2,1)} %bitcast.25), calls=%async_computation.2 | async-start | bytes 1572864 | tf_op jit(solution)/shard_map/all_to_all | solution.py:229
  1525.3 3.5 copy-start.19
  1526.9 3.3 copy-start.18
  1530.2 2.5 copy-start.17
  1532.7 2.5 copy-start.16
  1535.2 10.7 slice-start
  1536.6 9.3 slice-start.1
  1536.6 9.3 slice-start.2
  (12 other events, 13.5 us)
Sparse Core Ops, SparseCore 0:
  207.6 955.2 all-reduce.8
  1168.1 357.1 all-reduce.6
